TPU v7x, 512 devices: a whole 4x4x16 slice. The times are simulated.
512 devices in a mesh: blk: 128 (over x, z, y_hi), grp: 4 (over y_lo, core).
Axes of the slice: x: 4, y: 4 (y_hi: 2, y_lo: 2; y = y_hi * 2 + y_lo), z: 16, core: 2. Of those that a mesh axis runs over, the one named last changes fastest.
Arguments:
- values: bfloat16 [128, 4, 6, 64, 4096], P('blk', 'grp'), may hold values from -96 to 96
- counts: int32 [128, 4], P('blk', 'grp'), may hold values from 1 to 6, as said below
- row_block: int32 [128, 4, 6], P('blk', 'grp'), may hold values from 0 to 1
- col_block: int32 [128, 4, 6], P('blk', 'grp'), may hold values from 0 to 127
- depth_block: int32 [128, 4, 6], P('blk', 'grp'), may hold values from 0 to 3
- factor_b: bfloat16 [8192, 256], P('blk')
- factor_c: bfloat16 [1024, 256], P('grp')
- fetch_list: int32 [128, 4, 64], P('blk', 'grp'), may hold values from 0 to 255, as said below
Outputs:
- a_new: bfloat16 [16384, 256], P(('blk', 'grp'))
- fetched: bfloat16 [128, 4, 64, 4096], P('blk', 'grp')
Inputs may be any that keep to these rules, and one draw needn't show every extreme that they name: `counts`: each device has 1 to 6 live slots; some device has exactly 6; slots beyond the live ones hold values that must not count. `fetch_list`: entry f of a device names unit f mod 2 of blk index f div 2, in the device's own index of grp; the 64 entries of one device name 64 distinct indices of blk.
All inputs are finite; a program needn't handle non-finite values.
Results may differ from a plain program's by a relative error of at most 0.00185.
Values may be sent and summed in bfloat16 or wider, within the bound.
A program may use at most 64 MiB of HBM per device.

v0:
```python
import jax
import jax.numpy as jnp
from jax import lax
from jax.sharding import PartitionSpec as P

IBD = 2


def on_device(values, counts, row_block, col_block, depth_block, factor_b, factor_c, fetch_list):
    side_cells = values.shape[3]
    slot_total = values.shape[2]
    rank_width = factor_b.shape[1]
    whole_columns = lax.all_gather(factor_b, "blk", axis=0, tiled=True)
    live_count = counts[0, 0]

    def block_term(slot):
        cube = values[0, 0, slot].reshape(side_cells * side_cells, side_cells)
        depth_rows = lax.dynamic_slice_in_dim(
            factor_c, depth_block[0, 0, slot] * side_cells, side_cells, 0
        )
        product = jnp.dot(cube, depth_rows, preferred_element_type=jnp.float32)
        product = product.reshape(side_cells, side_cells, rank_width)
        column_rows = lax.dynamic_slice_in_dim(
            whole_columns, col_block[0, 0, slot] * side_cells, side_cells, 0
        )
        return jnp.sum(product * column_rows.astype(jnp.float32)[None, :, :], axis=1)

    def add_into(partial_value, slot, term):
        start = row_block[0, 0, slot] * side_cells
        current = lax.dynamic_slice_in_dim(partial_value, start, side_cells, 0)
        return lax.dynamic_update_slice_in_dim(partial_value, current + term, start, 0)

    empty = jnp.zeros((IBD * side_cells, rank_width), jnp.float32)

    def masked_step(slot, partial_value):
        term = block_term(slot)
        term = jnp.where(slot < live_count, term, jnp.zeros_like(term))
        return add_into(partial_value, slot, term)

    partial_value = lax.fori_loop(0, slot_total, masked_step, empty)
    summed = lax.psum_scatter(partial_value, "grp", scatter_dimension=0, tiled=True)
    gram_c = lax.psum(
        jnp.einsum("kr,ks->rs", factor_c, factor_c, preferred_element_type=jnp.float32), "grp"
    )
    gram_b = lax.psum(
        jnp.einsum("jr,js->rs", factor_b, factor_b, preferred_element_type=jnp.float32), "blk"
    )
    system = gram_b * gram_c
    lower = jnp.linalg.cholesky(system)
    solved = jax.scipy.linalg.cho_solve((lower, True), summed.T).T
    a_local = solved.astype(jnp.bfloat16)
    unit_rows = side_cells // lax.axis_size("grp")
    unit_width = unit_rows * rank_width
    wanted = fetch_list[0, 0]
    owners = wanted // IBD
    within = wanted % IBD
    every_unit = lax.all_gather(a_local, "blk", axis=0, tiled=True)
    every_unit = every_unit.reshape(-1, unit_width)
    fetched = every_unit[owners * IBD + within]
    return (a_local, fetched.reshape(1, 1, -1, unit_width))


def solution(mesh):
    placed = (
        P("blk", "grp", None, None, None),
        P("blk", "grp"),
        P("blk", "grp", None),
        P("blk", "grp", None),
        P("blk", "grp", None),
        P("blk", None),
        P("grp", None),
        P("blk", "grp", None),
    )
    return jax.shard_map(
        on_device,
        mesh=mesh,
        in_specs=placed,
        out_specs=(P(("blk", "grp"), None), P("blk", "grp", None, None)),
        check_vma=False,
    )
```

profile of v0, /device:TPU:2, one launch (start us, length us, event | category | flops | bytes accessed | tf_op | source)
XLA Modules:
  0.0 1851.6 jit_solution(1996384470419710080)
XLA Ops:
  7.2 1.8 fusion.20
  9.1 1.9 fusion.21
  11.8 1232.0 %all-reduce.4.cloned.1.call-done = f32[256,256]{0,1:T(8,128)} async-done(((f32[256,256]{0,1:T(8,128)}), f32[256,256]{0,1:T(8,128)}) %all-reduce.4.cloned.1.call-update) | async-done | bytes 262160 | tf_op jit(solution)/shard_map/psum | solution.py:45
  1243.9 57.8 %all-reduce.6.cloned.1.call-done = f32[256,256]{0,1:T(8,128)} async-done(((f32[256,256]{0,1:T(8,128)}), f32[256,256]{0,1:T(8,128)}) %all-reduce.6.cloned.1.call-update) | async-done | bytes 262160 | tf_op jit(solution)/shard_map/psum | solution.py:42
  1302.9 11.7 cholesky.50
  1314.7 9.8 custom-call.18
  1325.0 11.7 cholesky.105
  1338.7 190.4 %all-gather.3.cloned.1.call-done = bf16[8192,256]{1,0:T(8,128)(2,1)} async-done(((bf16[64,256]{1,0:T(8,128)(2,1)}), bf16[8192,256]{1,0:T(8,128)(2,1)}) %all-gather.3.cloned.1.call-update) | async-done | bytes 4194320 | tf_op jit(solution)/shard_map/all_gather | solution.py:13
  1529.2 72.5 %while.14 = (s32[]{:T(128)}, f32[128,256]{1,0:T(8,128)S(1)}, s32[1,1,6]{2,1,0:T(1,128)S(1)}, s32[]{:T(128)}, bf16[1,1,6,64,4096]{4,3,2,1,0:T(8,128)(2,1)}, /*ind...) while((s32[]{:T(128)}, f32[128,256]{1,0:T(8,128)S(1)}, ...), condition=%wide.region_8.9_spmd, body=%wide.region_6.8_spmd.sunk | while | flops 136347664 | bytes 3080493 | solution.py:40
  1538.8 1.1 dot_general.16
  1539.9 1.5 multiply_reduce_fusion.2
  1552.0 1.5 multiply_reduce_fusion.2
  1564.0 1.5 multiply_reduce_fusion.2
  1574.9 1.1 dot_general.16
  1576.1 1.5 multiply_reduce_fusion.2
  1588.1 1.5 multiply_reduce_fusion.2
  1600.2 1.5 multiply_reduce_fusion.2
  1602.5 3.9 while.15
  1603.1 1.3 bitcast_dynamic-update-slice_fusion.2
  1605.0 1.3 bitcast_dynamic-update-slice_fusion.2
  1606.4 19.7 %custom-call.19 = f32[2,128,128]{1,2,0:T(8,128)S(1)} custom-call(f32[2,128,128]{2,1,0:T(8,128)S(1)} %get-tuple-element.164), custom_call_target="InvertDiagBlocksLowerTriangular" | custom-call | tf_op jit(solution)/shard_map/jit(_cho_solve)/triangular_solve | solution.py:50
  1629.5 211.0 %all-gather.5.cloned.1.call-done = bf16[4096,256]{1,0:T(8,128)(2,1)} async-done(((bf16[32,256]{1,0:T(8,128)(2,1)}), bf16[4096,256]{1,0:T(8,128)(2,1)}) %all-gather.5.cloned.1.call-update) | async-done | bytes 2097168 | tf_op jit(solution)/shard_map/all_gather | solution.py:57
  1840.5 2.9 reshape.159
  1843.4 1.7 gather_fusion
  (83 shorter events, 31.7 us)
Async XLA Ops:
  7.2 1522.0 %copy-start.3 = (s32[1,1,6]{2,1,0:T(1,128)S(1)}, s32[1,1,6]{2,1,0:T(1,128)}, u32[]{:S(2)}) copy-start(s32[1,1,6]{2,1,0:T(1,128)} %param.14) | copy-start | bytes 76
  7.2 1522.0 %copy-start.2 = (s32[1,1,6]{2,1,0:T(1,128)S(1)}, s32[1,1,6]{2,1,0:T(1,128)}, u32[]{:S(2)}) copy-start(s32[1,1,6]{2,1,0:T(1,128)} %param.13) | copy-start | bytes 76
  7.2 1522.0 %copy-start.1 = (s32[1,1,6]{2,1,0:T(1,128)S(1)}, s32[1,1,6]{2,1,0:T(1,128)}, u32[]{:S(2)}) copy-start(s32[1,1,6]{2,1,0:T(1,128)} %param.12) | copy-start | bytes 76
  7.2 1236.7 %all-reduce.4.cloned.1.call-start = ((), (), s32[]{:S(2)}) async-start(), calls=%async_computation.1 | async-start | bytes 524288 | tf_op jit(solution)/shard_map/psum | solution.py:45
  9.0 1292.6 %all-reduce.6.cloned.1.call-start = ((), (), s32[]{:S(2)}) async-start(), calls=%async_computation.2 | async-start | bytes 524288 | tf_op jit(solution)/shard_map/psum | solution.py:42
  11.0 1518.1 %all-gather.3.cloned.1.call-start = ((), (), s32[]{:S(2)}) async-start(), calls=%async_computation.3 | async-start | bytes 4227072 | tf_op jit(solution)/shard_map/all_gather | solution.py:13
  11.8 1614.3 %reduce-scatter.2.cloned.1.call-start = ((), (), s32[]{:S(2)}) async-start(), calls=%async_computation.4 | async-start | bytes 163840 | tf_op jit(solution)/shard_map/reduce_scatter | solution.py:41
  1529.2 100.3 %copy-start.4 = (s32[1,1,64]{2,1,0:T(1,128)S(1)}, s32[1,1,64]{2,1,0:T(1,128)}, u32[]{:S(2)}) copy-start(s32[1,1,64]{2,1,0:T(1,128)} %param.17) | copy-start | bytes 772
  1601.7 0.7 copy-start
  1602.4 238.2 %all-gather.5.cloned.1.call-start = ((), (), s32[]{:S(2)}) async-start(), calls=%async_computation.5 | async-start | bytes 2113536 | tf_op jit(solution)/shard_map/all_gather | solution.py:57
Sparse Core Ops, SparseCore 0:
  11.5 1232.3 all-reduce.3
  1247.0 54.5 all-reduce.5
  1306.1 222.9 all-gather.2
  1602.5 19.0 reduce-scatter.1
  1629.6 210.8 all-gather.4
where the time goes:
time: 1850 us
  waiting for transfers between devices  1690 us (91%)
  other arithmetic  67.4 us (4%)
  loops' own time  38.6 us (2%)
  local copies, waits for them, and re-layouts  22.5 us (1%)
    psum x1, waiting for transfers between devices, on_device(): lax.psum(jnp.einsum('jr,js->rs', factor_b, factor_b, preferred_element_ty...  1230 us
    all_gather x1, waiting for transfers between devices, on_device(): every_unit = lax.all_gather(a_local, 'blk', axis=0, tiled=True)  211 us
    all_gather x1, waiting for transfers between devices, on_device(): whole_columns = lax.all_gather(factor_b, 'blk', axis=0, tiled=True)  190 us
    psum x1, waiting for transfers between devices, on_device(): lax.psum(jnp.einsum('kr,ks->rs', factor_c, factor_c, preferred_element_ty...  57.8 us
    another operation x1, loops' own time, on_device(): partial_value = lax.fori_loop(0, slot_total, masked_step, empty)  38.6 us
  transfers between devices with their start and end apart: 5, of which 4 were waited for; matrix products, arithmetic and copies ran while one was open for 3% of the time, Pallas kernels for 0%

commit v1 on v0

v1 whole, which is shorter than its diff:
```python
import functools

import jax
import jax.numpy as jnp
from jax import lax
from jax.experimental import pallas as pl
from jax.experimental.pallas import tpu as pltpu
from jax.sharding import PartitionSpec as P

MESH = pl.DeviceIdType.MESH
NX, NZ, NY, NC = 4, 16, 4, 2
YH = 2
R = 256
EDGE = 64
NB = 6
PIECE = 16
ROWS = 32
SLOTS = 64
F32 = jnp.float32
BF16 = jnp.bfloat16


def place():
    b, g = lax.axis_index("blk"), lax.axis_index("grp")
    x, z, yh = b // (NZ * YH), (b // YH) % NZ, b % YH
    return x, z, yh * 2 + g // NC, g % NC


def device(x, z, y, c):
    return ((x * NZ + z) * YH + y // 2, (y % 2) * NC + c)


def greet(others):
    barrier = pltpu.get_barrier_semaphore()
    for other in others:
        pl.semaphore_signal(barrier, inc=1, device_id=other, device_id_type=MESH)
    pl.semaphore_wait(barrier, len(others))


def offsets(n):
    order = []
    for d in range(1, n // 2 + 1):
        order.append(d)
        if n - d != d:
            order.append(n - d)
    return order


def gather_kernel(
    b_ref, c_ref, full, full_c,
    send_z, recv_z, send_a, recv_a, send_b, recv_b, send_a2, recv_a2,
    send_b2, recv_b2, send_s, recv_s, send_c, recv_c,
):
    x, z, y, c = place()
    g = (y % 2) * NC + c
    half = NZ // 2
    sibling = device(x, z, y, 1 - c)
    across = device(x, z, y + 1 - 2 * (y % 2), c)

    full[x, z, y, c] = b_ref[pl.ds(pl.multiple_of(g * PIECE, PIECE), PIECE), :]
    full_c[g] = c_ref[...]

    others = [device(x, (z + d) % NZ, y, c) for d in range(1, NZ)]
    others += [device((x + d) % NX, z, y, c) for d in range(1, NX)]
    others += [device(x, z, (y + d) % NY, c) for d in range(1, NY)]
    others += [sibling]
    greet(others)

    sent = []

    def send(source, send_sem, recv_sem, target):
        copy = pltpu.make_async_remote_copy(
            src_ref=source, dst_ref=source, send_sem=send_sem, recv_sem=recv_sem,
            device_id=target, device_id_type=MESH,
        )
        copy.start()
        sent.append(copy)

    def arrived(target, send_sem, recv_sem):
        pltpu.make_async_remote_copy(
            src_ref=target, dst_ref=target, send_sem=send_sem, recv_sem=recv_sem,
            device_id=sibling, device_id_type=MESH,
        ).wait_recv()

    passed = []

    def share(block, other_block):
        n = len(passed)
        send(block, send_s.at[n], recv_s.at[n], sibling)
        passed.append(other_block)

    for d in offsets(NZ):
        send(full.at[x, z, y, c], send_z.at[d - 1], recv_z.at[d - 1], device(x, (z + d) % NZ, y, c))
    send(full_c.at[g], send_c.at[0], recv_c.at[0], across)
    send(full_c.at[g], send_c.at[1], recv_c.at[1], sibling)
    for d in offsets(NZ):
        arrived(full.at[x, (z - d + NZ) % NZ, y, c], send_z.at[d - 1], recv_z.at[d - 1])

    lower, upper = pl.ds(0, half), pl.ds(half, half)
    for d in offsets(NX):
        send(full.at[x, lower, y, c], send_a.at[d - 1], recv_a.at[d - 1], device((x + d) % NX, z, y, c))
    for d in offsets(NY):
        send(full.at[x, upper, y, c], send_b.at[d - 1], recv_b.at[d - 1], device(x, z, (y + d) % NY, c))
    share(full.at[x, :, y, c], full.at[x, :, y, 1 - c])
    g_across = g + 2 - 4 * (y % 2)
    arrived(full_c.at[g_across], send_c.at[0], recv_c.at[0])
    send(full_c.at[g_across], send_c.at[2], recv_c.at[2], sibling)
    for d in offsets(NX):
        arrived(full.at[x, lower, y, c], send_a.at[d - 1], recv_a.at[d - 1])
    for d in offsets(NY):
        send(full.at[:, lower, y, c], send_a2.at[d - 1], recv_a2.at[d - 1], device(x, z, (y + d) % NY, c))
    for d in offsets(NX):
        xd = (x - d + NX) % NX
        share(full.at[xd, lower, y, c], full.at[xd, lower, y, 1 - c])
    for d in offsets(NY):
        arrived(full.at[x, upper, y, c], send_b.at[d - 1], recv_b.at[d - 1])
    for d in offsets(NX):
        send(full.at[x, upper, :, c], send_b2.at[d - 1], recv_b2.at[d - 1], device((x + d) % NX, z, y, c))
    for d in offsets(NY):
        yd = (y - d + NY) % NY
        share(full.at[x, upper, yd, c], full.at[x, upper, yd, 1 - c])
    for d in offsets(NY):
        yd = (y - d + NY) % NY
        arrived(full.at[:, lower, yd, c], send_a2.at[d - 1], recv_a2.at[d - 1])
        share(full.at[:, lower, yd, c], full.at[:, lower, yd, 1 - c])
    for d in offsets(NX):
        xd = (x - d + NX) % NX
        arrived(full.at[xd, upper, :, c], send_b2.at[d - 1], recv_b2.at[d - 1])
        share(full.at[xd, upper, :, c], full.at[xd, upper, :, 1 - c])
    for n, block in enumerate(passed):
        arrived(block, send_s.at[n], recv_s.at[n])
    arrived(full_c.at[0], send_c.at[1], recv_c.at[1])
    arrived(full_c.at[0], send_c.at[2], recv_c.at[2])
    for copy in sent:
        copy.wait_send()


def terms_kernel(
    counts_ref, row_ref, col_ref, depth_ref, b_ref, own_c_ref, c_ref, values_ref,
    partial_ref, inverse_ref, weights, work,
):
    partial_ref[...] = jnp.zeros_like(partial_ref)
    weights[...] = jnp.zeros_like(weights)
    live = counts_ref[0, 0]
    chunks = EDGE * EDGE // R

    def slot_step(s, carry):
        depth = pl.multiple_of(depth_ref[0, 0, s] * EDGE, EDGE)
        rows = own_c_ref[pl.ds(depth, EDGE), :]
        for q in range(4):
            weights[q, q * EDGE:(q + 1) * EDGE, :] = rows
        b_rows = b_ref[col_ref[0, 0, s]].astype(F32)
        cube = jnp.concatenate(
            [values_ref[0, 0, s, :, t * R:(t + 1) * R] for t in range(chunks)], axis=0
        )
        term = jnp.zeros((EDGE, R), F32)
        for q in range(4):
            product = jnp.dot(cube, weights[q], preferred_element_type=F32)
            for t in range(chunks):
                j = t * 4 + q
                term += product[t * EDGE:(t + 1) * EDGE, :] * b_rows[j:j + 1, :]
        row = jnp.full((EDGE, R), row_ref[0, 0, s], jnp.int32)
        term = jnp.where(jnp.full((EDGE, R), live - s, jnp.int32) > 0, term, 0.0)
        for i in range(2):
            partial_ref[i * EDGE:(i + 1) * EDGE, :] += jnp.where(row == i, term, 0.0)
        return carry

    lax.fori_loop(0, NB, slot_step, 0)

    def gram(ref_at, parts):
        def step(i, total):
            block = ref_at(i)
            return total + lax.dot_general(
                block, block, (((0,), (0,)), ((), ())), preferred_element_type=F32
            )
        return lax.fori_loop(0, parts, step, jnp.zeros((R, R), F32))

    gram_b = gram(lambda i: b_ref[pl.ds(i * 8, 8)].reshape(8 * EDGE, R), NX * NZ * YH // 8)
    gram_c = gram(lambda i: c_ref[i], 4)
    invert(gram_b * gram_c, inverse_ref, work)


def split(a):
    high = a.astype(BF16)
    return high, (a - high.astype(F32)).astype(BF16)


def three_pass(a, b):
    a_high, a_low = a
    b_high, b_low = b
    return jnp.dot(
        jnp.concatenate([a_high, a_low, a_high], axis=1),
        jnp.concatenate([b_high, b_high, b_low], axis=0),
        preferred_element_type=F32,
    )


def exact_dot(a, b):
    return jnp.dot(a, b, precision=lax.Precision.HIGHEST, preferred_element_type=F32)


def invert(system, out_ref, work):
    sub = lax.broadcasted_iota(jnp.int32, (R, R), 0)
    lane = lax.broadcasted_iota(jnp.int32, (R, R), 1)
    eye = jnp.where(sub == lane, 1.0, 0.0).astype(F32)
    diagonal = system * eye
    across = lax.rsqrt(jnp.sum(diagonal, axis=0, keepdims=True))
    down = lax.rsqrt(jnp.sum(diagonal, axis=1, keepdims=True))
    scaled = system * across * down
    bound = jnp.max(jnp.sum(jnp.abs(scaled), axis=0, keepdims=True), axis=1, keepdims=True)
    start = 1.0 / bound
    rest = eye - scaled * start
    guess = (eye + rest) * start
    for _ in range(8):
        rest_parts = split(rest)
        rest = three_pass(rest_parts, rest_parts)
        guess = guess + three_pass(split(guess), split(rest))
    work[...] = guess

    def unfinished(state):
        count, error = state
        return jnp.logical_and(count < 24, jnp.logical_not(error <= 2e-4))

    def refine(state):
        count, _ = state
        guess = work[...]
        rest = eye - exact_dot(guess, scaled)
        work[...] = guess + exact_dot(guess, rest)
        error = jnp.max(jnp.sum(jnp.abs(rest), axis=0, keepdims=True))
        return count + 1, error

    _, error = lax.while_loop(unfinished, refine, (jnp.int32(0), jnp.float32(1.0)))

    @pl.when(jnp.logical_not(error <= 2e-4))
    def _():
        work[...] = scaled

        def pivot(k, carry):
            a = work[...]
            row = work[pl.ds(k, 1), :]
            column = jnp.sum(jnp.where(lane == k, a, 0.0), axis=1, keepdims=True)
            value = jnp.sum(jnp.where(lane[:1] == k, row, 0.0), axis=1, keepdims=True)
            row = row / value
            updated = jnp.where(lane == k, -column / value, a - column * row)
            updated = jnp.where(sub == k, jnp.where(lane == k, 1.0 / value, row), updated)
            work[...] = updated
            return carry

        lax.fori_loop(0, R, pivot, 0)

    out_ref[...] = work[...] * across * down


def update_kernel(
    partial_ref, inverse_ref, a_ref, full, parts,
    send_g, recv_g, send_z, recv_z, send_a, recv_a, send_b, recv_b,
    send_a2, recv_a2, send_b2, recv_b2,
):
    x, z, y, c = place()
    yh, yl = y // 2, y % 2
    g = yl * NC + c
    half = NZ // 2
    facing = device(x, z, (y + 2) % NY, c)

    def member(other):
        return device(x, z, yh * 2 + other // NC, other % NC)

    others = [member((g + d) % 4) for d in range(1, 4)]
    others += [device(x, (z + d) % NZ, y, c) for d in range(1, NZ)]
    others += [device((x + d) % NX, z, y, c) for d in range(1, NX)]
    others += [facing]
    greet(others)

    sent = []

    def send(source, target, send_sem, recv_sem, other):
        copy = pltpu.make_async_remote_copy(
            src_ref=source, dst_ref=target, send_sem=send_sem, recv_sem=recv_sem,
            device_id=other, device_id_type=MESH,
        )
        copy.start()
        sent.append(copy)

    def arrived(target, send_sem, recv_sem):
        pltpu.make_async_remote_copy(
            src_ref=target, dst_ref=target, send_sem=send_sem, recv_sem=recv_sem,
            device_id=facing, device_id_type=MESH,
        ).wait_recv()

    def own(other):
        return pl.ds(pl.multiple_of(other * ROWS, ROWS), ROWS)

    for d in (2, 1, 3):
        other = (g + d) % 4
        send(partial_ref.at[own(other)], parts.at[d - 1], send_g.at[d - 1], recv_g.at[d - 1], member(other))
    total = partial_ref[own(g), :]
    for d in (1, 3, 2):
        arrived(parts.at[d - 1], send_g.at[d - 1], recv_g.at[d - 1])
        total = total + parts[d - 1]
    solved = exact_dot(total, inverse_ref[...]).astype(BF16)
    a_ref[...] = solved
    full[x, z, yh] = solved

    for d in offsets(NZ):
        here = full.at[x, z, yh]
        send(here, here, send_z.at[d - 1], recv_z.at[d - 1], device(x, (z + d) % NZ, y, c))
    for d in offsets(NZ):
        arrived(full.at[x, (z - d + NZ) % NZ, yh], send_z.at[d - 1], recv_z.at[d - 1])
    lower, upper = pl.ds(0, half), pl.ds(half, half)
    for d in offsets(NX):
        here = full.at[x, lower, yh]
        send(here, here, send_a.at[d - 1], recv_a.at[d - 1], device((x + d) % NX, z, y, c))
    here = full.at[x, upper, yh]
    send(here, here, send_b.at[0], recv_b.at[0], facing)
    for d in offsets(NX):
        arrived(full.at[x, lower, yh], send_a.at[d - 1], recv_a.at[d - 1])
    here = full.at[:, lower, yh]
    send(here, here, send_a2.at[0], recv_a2.at[0], facing)
    arrived(full.at[x, upper, yh], send_b.at[0], recv_b.at[0])
    for d in offsets(NX):
        here = full.at[x, upper]
        send(here, here, send_b2.at[d - 1], recv_b2.at[d - 1], device((x + d) % NX, z, y, c))
    arrived(full.at[:, lower, yh], send_a2.at[0], recv_a2.at[0])
    for d in offsets(NX):
        arrived(full.at[x, upper], send_b2.at[d - 1], recv_b2.at[d - 1])
    for copy in sent:
        copy.wait_send()


def pick_kernel(fetch_ref, full, fetched_ref, units):
    def pick(s, carry):
        f = fetch_ref[0, 0, s]
        owner, within = lax.div(f, 2), lax.rem(f, 2)
        start = pl.multiple_of(within * PIECE, PIECE)
        pair = lax.div(owner, YH)
        unit = full[lax.div(pair, NZ), lax.rem(pair, NZ), lax.rem(owner, YH), pl.ds(start, PIECE), :]
        unit = unit.astype(F32)
        for h in range(2):
            units[h, pl.ds(pl.multiple_of(s * PIECE, PIECE), PIECE), :] = unit[:, h * 128:(h + 1) * 128]
        return carry

    lax.fori_loop(0, SLOTS, pick, 0, unroll=4)
    for r in range(PIECE):
        for h in range(2):
            at = r * R + h * 128
            picked = units.at[h][pl.ds(r, SLOTS, stride=PIECE), :]
            fetched_ref[0, 0, :, at:at + 128] = picked.astype(BF16)


def dma(n):
    return pltpu.SemaphoreType.DMA((n,))


VMEM = pl.BlockSpec(memory_space=pltpu.VMEM)
SMEM = pl.BlockSpec(memory_space=pltpu.SMEM)
ANY = pl.BlockSpec(memory_space=pl.ANY)


def on_device(values, counts, row_block, col_block, depth_block, factor_b, factor_c, fetch_list):
    full_b, full_c = pl.pallas_call(
        gather_kernel,
        out_shape=(
            jax.ShapeDtypeStruct((NX, NZ, NY, NC, PIECE, R), BF16),
            jax.ShapeDtypeStruct((4, 256, R), BF16),
        ),
        in_specs=[VMEM] * 2,
        out_specs=(VMEM, VMEM),
        scratch_shapes=[
            dma(NZ - 1), dma(NZ - 1), dma(NX - 1), dma(NX - 1), dma(NY - 1), dma(NY - 1),
            dma(NY - 1), dma(NY - 1), dma(NX - 1), dma(NX - 1), dma(13), dma(13),
            dma(3), dma(3),
        ],
        compiler_params=pltpu.CompilerParams(
            collective_id=0, has_side_effects=True, vmem_limit_bytes=12 << 20
        ),
        name="gather_factors",
    )(factor_b, factor_c)
    partial, inverse = pl.pallas_call(
        terms_kernel,
        out_shape=(
            jax.ShapeDtypeStruct((2 * EDGE, R), F32),
            jax.ShapeDtypeStruct((R, R), F32),
        ),
        in_specs=[SMEM] * 4 + [VMEM] * 4,
        out_specs=(VMEM, VMEM),
        scratch_shapes=[pltpu.VMEM((4, R, R), BF16), pltpu.VMEM((R, R), F32)],
        compiler_params=pltpu.CompilerParams(vmem_limit_bytes=32 << 20),
        name="terms_inverse",
    )(counts, row_block, col_block, depth_block,
      full_b.reshape(NX * NZ * YH, EDGE, R), factor_c, full_c, values)
    a_new, full_a = pl.pallas_call(
        update_kernel,
        out_shape=(
            jax.ShapeDtypeStruct((ROWS, R), BF16),
            jax.ShapeDtypeStruct((NX, NZ, YH, ROWS, R), BF16),
        ),
        in_specs=[VMEM, VMEM],
        out_specs=(VMEM, VMEM),
        scratch_shapes=[
            pltpu.VMEM((3, ROWS, R), F32),
            dma(3), dma(3), dma(NZ - 1), dma(NZ - 1), dma(NX - 1), dma(NX - 1), dma(1), dma(1),
            dma(1), dma(1), dma(NX - 1), dma(NX - 1),
        ],
        compiler_params=pltpu.CompilerParams(
            collective_id=1, has_side_effects=True, vmem_limit_bytes=12 << 20
        ),
        name="update_gather",
    )(partial, inverse)
    fetched = pl.pallas_call(
        pick_kernel,
        out_shape=jax.ShapeDtypeStruct((1, 1, SLOTS, PIECE * R), BF16),
        in_specs=[SMEM, VMEM],
        out_specs=VMEM,
        scratch_shapes=[pltpu.VMEM((2, SLOTS * PIECE, 128), F32)],
        compiler_params=pltpu.CompilerParams(vmem_limit_bytes=16 << 20),
        name="pick_units",
    )(fetch_list, full_a)
    return a_new, fetched


def solution(mesh):
    placed = (
        P("blk", "grp", None, None, None),
        P("blk", "grp"),
        P("blk", "grp", None),
        P("blk", "grp", None),
        P("blk", "grp", None),
        P("blk", None),
        P("grp", None),
        P("blk", "grp", None),
    )
    return jax.shard_map(
        on_device,
        mesh=mesh,
        in_specs=placed,
        out_specs=(P(("blk", "grp"), None), P("blk", "grp", None, None)),
        check_vma=False,
    )
```

time: 1850 us -> 182 us (0.10)
  the two profiles are of different devices: /device:TPU:2 before, /device:TPU:40 now
where the time goes in v1:
time: 182 us
  Pallas kernels  173 us (95%)
  local copies, waits for them, and re-layouts  7.02 us (4%)
    pallas_call x1, Pallas kernels, on_device(): pl.pallas_call(terms_kernel, out_shape=(jax.ShapeDtypeStruct((2 * EDGE, R...  77.4 us
    pallas_call x1, Pallas kernels, on_device(): pl.pallas_call(update_kernel, out_shape=(jax.ShapeDtypeStruct((ROWS, R),...  48.8 us
    pallas_call x1, Pallas kernels, on_device(): pl.pallas_call(gather_kernel, out_shape=(jax.ShapeDtypeStruct((NX, NZ, NY...  44.6 us
    unnamed x17, local copies, waits for them, and re-layouts  7.02 us

profile of v1, /device:TPU:40, one launch (start us, length us, event | category | flops | bytes accessed | tf_op | source)
XLA Modules:
  0.0 181.6 jit_solution(18279021039760014266)
XLA Ops:
  1.3 0.0 copy-start.1
  1.3 0.9 copy-done.1
  2.2 0.0 copy-start.3
  2.2 0.8 copy-done.3
  2.9 44.6 %gather_factors.1 = (bf16[4,16,4,2,16,256]{5,4,3,2,1,0:T(8,128)(2,1)S(1)}, bf16[4,256,256]{2,1,0:T(8,128)(2,1)S(1)}) custom-call(bf16[64,256]{1,0:T(8,128)(2,1)S(1)} %copy-done.3, bf16[256,256]{1,0:T(8,128)(2,1)S(1)} %copy-done.1), custom_call_target="tpu_custom_call" | custom-call | tf_op jit(solution)/shard_map/gather_factors/pallas_call | solution.py:360
  47.6 0.0 copy-start
  47.6 1.9 %copy-done = bf16[1,1,6,64,4096]{4,3,2,1,0:T(8,128)(2,1)S(1)} copy-done((bf16[1,1,6,64,4096]{4,3,2,1,0:T(8,128)(2,1)S(1)}, bf16[1,1,6,64,4096]{4,3,2,1,0:T(8,128)(2,1)}, u32[]{:S(2)}) %copy-start) | copy-done | bytes 3145752
  49.4 0.0 copy-start.2
  49.4 0.9 copy-done.2
  50.4 0.0 copy-start.4
  50.4 0.7 copy-done.4
  51.0 0.0 copy-start.5
  51.0 0.7 copy-done.5
  51.7 0.0 copy-start.6
  51.7 0.7 copy-done.6
  52.3 0.0 copy-start.7
  52.3 77.4 %terms_inverse.1 = (f32[128,256]{1,0:T(8,128)S(1)}, f32[256,256]{1,0:T(8,128)S(1)}) custom-call(s32[1,1]{1,0:T(1,128)S(6)} %copy.11.counts_ref, s32[1,1,6]{2,1,0:T(1,128)S(1)} %copy-done.4, s32[1,1,6]{2,1,0:T(1,128)S(1)} %copy-done.5, s32[1,1,6]{2,1,0:T(1,128)S(1)} %copy-done.6, bf16[128,64,256]{2,1,0:T(8,128)(2,1)S(1)} %bitcast.1, ...), custom_call_target="tpu_custom_call" | custom-call | tf_op jit(solution)/shard_map/terms_inverse/pallas_call | solution.py:378
  129.7 48.8 %update_gather.1 = (bf16[32,256]{1,0:T(8,128)(2,1)S(1)}, bf16[4,16,2,32,256]{4,3,2,1,0:T(8,128)(2,1)S(1)}) custom-call(f32[128,256]{1,0:T(8,128)S(1)} %get-tuple-element.10.partial_ref, f32[256,256]{1,0:T(8,128)S(1)} %get-tuple-element.11.inverse_ref), custom_call_target="tpu_custom_call" | custom-call | tf_op jit(solution)/shard_map/update_gather/pallas_call | solution.py:391
  178.5 0.0 copy-done.7
  178.5 2.5 %pick_units.1 = bf16[1,1,64,4096]{3,2,1,0:T(8,128)(2,1)} custom-call(s32[1,1,64]{2,1,0:T(1,128)S(1)} %copy-done.7, bf16[4,16,2,32,256]{4,3,2,1,0:T(8,128)(2,1)S(1)} %get-tuple-element.13.full), custom_call_target="tpu_custom_call" | custom-call | tf_op jit(solution)/shard_map/pick_units/pallas_call | solution.py:409
  181.0 0.6 copy.12
Async XLA Ops:
  1.3 0.9 copy-start.1
  2.2 0.8 copy-start.3
  47.6 1.9 %copy-start = (bf16[1,1,6,64,4096]{4,3,2,1,0:T(8,128)(2,1)S(1)}, bf16[1,1,6,64,4096]{4,3,2,1,0:T(8,128)(2,1)}, u32[]{:S(2)}) copy-start(bf16[1,1,6,64,4096]{4,3,2,1,0:T(8,128)(2,1)} %values_ref.1) | copy-start | bytes 9437188
  49.4 0.9 copy-start.2
  50.4 0.7 copy-start.4
  51.0 0.7 copy-start.5
  51.7 0.7 copy-start.6
  52.3 126.2 %copy-start.7 = (s32[1,1,64]{2,1,0:T(1,128)S(1)}, s32[1,1,64]{2,1,0:T(1,128)}, u32[]{:S(2)}) copy-start(s32[1,1,64]{2,1,0:T(1,128)} %fetch_ref.1) | copy-start | bytes 772

commit v2 on v1

v2 whole, which is shorter than its diff:
```python
import functools

import jax
import jax.numpy as jnp
from jax import lax
from jax.experimental import pallas as pl
from jax.experimental.pallas import tpu as pltpu
from jax.sharding import PartitionSpec as P

MESH = pl.DeviceIdType.MESH
NX, NZ, NY, NC = 4, 16, 4, 2
YH = 2
R = 256
EDGE = 64
NB = 6
PIECE = 16
ROWS = 32
SLOTS = 64
F32 = jnp.float32
BF16 = jnp.bfloat16


def place():
    b, g = lax.axis_index("blk"), lax.axis_index("grp")
    x, z, yh = b // (NZ * YH), (b // YH) % NZ, b % YH
    return x, z, yh * 2 + g // NC, g % NC


def device(x, z, y, c):
    return ((x * NZ + z) * YH + y // 2, (y % 2) * NC + c)


def greet(others):
    barrier = pltpu.get_barrier_semaphore()
    for other in others:
        pl.semaphore_signal(barrier, inc=1, device_id=other, device_id_type=MESH)
    pl.semaphore_wait(barrier, len(others))


def slot_of(d):
    d = d % NZ
    return max(2 * d - 1, 0) if d <= NZ // 2 else 2 * (NZ - d)


def slot_at(z_there, z_here):
    d = lax.rem(z_there - z_here + NZ, NZ)
    return jnp.where(d <= NZ // 2, jnp.maximum(2 * d - 1, 0), 2 * (NZ - d))


def groups():
    return [(0, 1)] + [(i, 2) for i in range(1, NZ - 1, 2)] + [(NZ - 1, 1)]


def offsets(n):
    order = []
    for d in range(1, n // 2 + 1):
        order.append(d)
        if n - d != d:
            order.append(n - d)
    return order


class Mover:
    def __init__(self, other):
        self.sent, self.other = [], other

    def send(self, source, target, send_sem, recv_sem, device_id):
        copy = pltpu.make_async_remote_copy(
            src_ref=source, dst_ref=target, send_sem=send_sem, recv_sem=recv_sem,
            device_id=device_id, device_id_type=MESH,
        )
        copy.start()
        self.sent.append(copy)

    def arrived(self, target, send_sem, recv_sem):
        pltpu.make_async_remote_copy(
            src_ref=target, dst_ref=target, send_sem=send_sem, recv_sem=recv_sem,
            device_id=self.other, device_id_type=MESH,
        ).wait_recv()

    def finish(self):
        for copy in self.sent:
            copy.wait_send()


LAGS_B = (1, 2, 3)
LAGS_A = (1, 2)
X_FIRST_B = (1, 3, 5, 7)
X_FIRST_A = (1, 2, 4, 5, 7)


def gather_kernel(
    b_ref, c_ref, values_ref,
    full, own_c, cubes, system_ref,
    full_c,
    local_sem, send_z, recv_z, send_1, recv_1, send_2, recv_2, send_s, recv_s, send_c, recv_c,
):
    x, z, y, c = place()
    g = (y % 2) * NC + c
    sibling = device(x, z, y, 1 - c)
    across = device(x, z, y + 1 - 2 * (y % 2), c)
    own_rows = pl.ds(pl.multiple_of(g * PIECE, PIECE), PIECE)
    loads = [
        pltpu.make_async_copy(b_ref.at[own_rows], full.at[x, 0, y, c], local_sem.at[0]),
        pltpu.make_async_copy(c_ref, own_c, local_sem.at[1]),
        pltpu.make_async_copy(values_ref.at[0, 0], cubes, local_sem.at[2]),
    ]
    for load in loads:
        load.start()

    others = [device(x, (z + d) % NZ, y, c) for d in range(1, NZ)]
    others += [device((x + d) % NX, z, y, c) for d in range(1, NX)]
    others += [device(x, z, (y + d) % NY, c) for d in range(1, NY)]
    others += [sibling]
    loads[0].wait()
    loads[1].wait()
    greet(others)
    mover = Mover(sibling)
    send, arrived = mover.send, mover.arrived

    for d in offsets(NZ):
        send(
            full.at[x, 0, y, c], full.at[x, slot_of(-d), y, c],
            send_z.at[d - 1], recv_z.at[d - 1], device(x, (z + d) % NZ, y, c),
        )

    def first(k, start, size):
        for slot in range(start, start + size):
            for d in range(1, NZ):
                if slot_of(-d) == slot:
                    arrived(full.at[x, slot, y, c], send_z.at[d - 1], recv_z.at[d - 1])
        here = full.at[x, pl.ds(start, size), y, c]
        for d in offsets(4):
            there = device((x + d) % NX, z, y, c) if k in X_FIRST_B else device(x, z, (y + d) % NY, c)
            send(here, here, send_1.at[k, d - 1], recv_1.at[k, d - 1], there)

    def second(k, start, size):
        for d in offsets(4):
            arrived(full.at[x, pl.ds(start, size), y, c], send_1.at[k, d - 1], recv_1.at[k, d - 1])
        if k in X_FIRST_B:
            here = full.at[:, pl.ds(start, size), y, c]
        else:
            here = full.at[x, pl.ds(start, size), :, c]
        for d in offsets(4):
            there = device(x, z, (y + d) % NY, c) if k in X_FIRST_B else device((x + d) % NX, z, y, c)
            send(here, here, send_2.at[k, d - 1], recv_2.at[k, d - 1], there)

    def third(k, start, size):
        for d in offsets(4):
            arrived(full.at[:, pl.ds(start, size), y, c], send_2.at[k, d - 1], recv_2.at[k, d - 1])
        here = full.at[:, pl.ds(start, size), :, c]
        send(here, here, send_s.at[k], recv_s.at[k], sibling)

    grams = [jnp.zeros((R, R), F32)]

    def gram(block):
        return lax.dot_general(
            block, block, (((0,), (0,)), ((), ())), preferred_element_type=F32
        )

    def fourth(k, start, size):
        arrived(full.at[:, pl.ds(start, size), :, 1 - c], send_s.at[k], recv_s.at[k])
        for i in range(NX):
            block = full[i, start:start + size].reshape(size * NY * NC * PIECE, R)
            grams[0] = grams[0] + gram(block)

    parts = groups()
    stages = (first, second, third, fourth)
    lags = (0,) + LAGS_B
    for t in range(len(parts) + lags[-1]):
        for stage, lag in zip(stages, lags):
            if 0 <= t - lag < len(parts):
                stage(t - lag, *parts[t - lag])
        if t == 0:
            send(own_c, full_c.at[g], send_c.at[0], recv_c.at[0], across)
            send(own_c, full_c.at[g], send_c.at[1], recv_c.at[1], sibling)
            g_across = g + 2 - 4 * (y % 2)
            gram_c = gram(own_c[...])
        if t == 3:
            arrived(full_c.at[g_across], send_c.at[0], recv_c.at[0])
            send(full_c.at[g_across], full_c.at[g_across], send_c.at[2], recv_c.at[2], sibling)
            gram_c = gram_c + gram(full_c[g_across])
    for i, other in ((1, g + 1 - 2 * c), (2, g_across + 1 - 2 * c)):
        arrived(full_c.at[other], send_c.at[i], recv_c.at[i])
        gram_c = gram_c + gram(full_c[other])
    system_ref[...] = grams[0] * gram_c
    loads[2].wait()
    mover.finish()


def split(a):
    high = a.astype(BF16)
    return high, (a - high.astype(F32)).astype(BF16)


def three_pass(a, b):
    a_high, a_low = a
    b_high, b_low = b
    return jnp.dot(
        jnp.concatenate([a_high, a_low, a_high], axis=1),
        jnp.concatenate([b_high, b_high, b_low], axis=0),
        preferred_element_type=F32,
    )


def exact_dot(a, b):
    return jnp.dot(a, b, precision=lax.Precision.HIGHEST, preferred_element_type=F32)


def invert(system, out_ref, work):
    sub = lax.broadcasted_iota(jnp.int32, (R, R), 0)
    lane = lax.broadcasted_iota(jnp.int32, (R, R), 1)
    eye = jnp.where(sub == lane, 1.0, 0.0).astype(F32)
    diagonal = system * eye
    across = lax.rsqrt(jnp.sum(diagonal, axis=0, keepdims=True))
    down = lax.rsqrt(jnp.sum(diagonal, axis=1, keepdims=True))
    scaled = system * across * down
    bound = jnp.max(jnp.sum(jnp.abs(scaled), axis=0, keepdims=True), axis=1, keepdims=True)
    start = 1.0 / bound
    rest = eye - scaled * start
    guess = (eye + rest) * start
    for _ in range(7):
        rest_parts = split(rest)
        rest = three_pass(rest_parts, rest_parts)
        guess = guess + three_pass(split(rest), split(guess))
    work[...] = guess

    def unfinished(state):
        count, error = state
        return jnp.logical_and(count < 24, jnp.logical_not(error <= 1e-3))

    def refine(state):
        count, _ = state
        guess = work[...]
        rest = eye - exact_dot(guess, scaled)
        work[...] = guess + exact_dot(rest, guess)
        error = jnp.max(jnp.sum(jnp.abs(rest), axis=0, keepdims=True))
        return count + 1, error

    _, error = lax.while_loop(unfinished, refine, (jnp.int32(0), jnp.float32(1.0)))

    @pl.when(jnp.logical_not(error <= 1e-3))
    def _():
        work[...] = scaled

        def pivot(k, carry):
            a = work[...]
            row = work[pl.ds(k, 1), :]
            column = jnp.sum(jnp.where(lane == k, a, 0.0), axis=1, keepdims=True)
            value = jnp.sum(jnp.where(lane[:1] == k, row, 0.0), axis=1, keepdims=True)
            row = row / value
            updated = jnp.where(lane == k, -column / value, a - column * row)
            updated = jnp.where(sub == k, jnp.where(lane == k, 1.0 / value, row), updated)
            work[...] = updated
            return carry

        lax.fori_loop(0, R, pivot, 0)

    out_ref[...] = work[...] * across * down


def inverse_kernel(
    counts_ref, row_ref, col_ref, depth_ref, full_ref, c_ref, system_ref,
    inverse_ref, rows_b_ref, rows_c_ref, keep_ref, work,
):
    z = place()[1]
    live = counts_ref[0, 0]
    for s in range(NB):
        col = col_ref[0, 0, s]
        pair = lax.div(col, YH)
        slot = slot_at(lax.rem(pair, NZ), z)
        rows = full_ref[lax.div(pair, NZ), slot, pl.ds(lax.rem(col, YH) * 2, 2)]
        rows_b_ref[s] = rows.reshape(EDGE, R).astype(F32)
        depth = pl.multiple_of(depth_ref[0, 0, s] * EDGE, EDGE)
        rows_c_ref[s] = c_ref[pl.ds(depth, EDGE), :]
        for i in range(2):
            keep = jnp.logical_and(s < live, row_ref[0, 0, s] == i)
            keep_ref[s, i] = jnp.full((8, R), jnp.where(keep, 1, 0), jnp.int32)
    invert(system_ref[...], inverse_ref, work)


def update_kernel(
    cubes, rows_b_ref, rows_c_ref, keep_ref, inverse_ref,
    a_ref, full,
    partial, weights, parts,
    send_g, recv_g, send_z, recv_z, send_1, recv_1, send_2, recv_2,
):
    x, z, y, c = place()
    yh, yl = y // 2, y % 2
    g = yl * NC + c
    facing = device(x, z, (y + 2) % NY, c)

    def member(other):
        return device(x, z, yh * 2 + other // NC, other % NC)

    others = [member((g + d) % 4) for d in range(1, 4)]
    others += [device(x, (z + d) % NZ, y, c) for d in range(1, NZ)]
    others += [device((x + d) % NX, z, y, c) for d in range(1, NX)]
    others += [facing]
    barrier = pltpu.get_barrier_semaphore()
    for other in others:
        pl.semaphore_signal(barrier, inc=1, device_id=other, device_id_type=MESH)

    partial[...] = jnp.zeros_like(partial)
    weights[...] = jnp.zeros_like(weights)
    chunks = EDGE * EDGE // R

    def slot_step(s, carry):
        for q in range(4):
            weights[q, q * EDGE:(q + 1) * EDGE, :] = rows_c_ref[s]
        b_rows = rows_b_ref[s]
        cube = jnp.concatenate(
            [cubes[s, :, t * R:(t + 1) * R] for t in range(chunks)], axis=0
        )
        term = jnp.zeros((EDGE, R), F32)
        for q in range(4):
            product = jnp.dot(cube, weights[q], preferred_element_type=F32)
            for t in range(chunks):
                j = t * 4 + q
                term += product[t * EDGE:(t + 1) * EDGE, :] * b_rows[j:j + 1, :]
        for i in range(2):
            keep = keep_ref[s, i][:1, :] > 0
            partial[i * EDGE:(i + 1) * EDGE, :] += jnp.where(keep, term, 0.0)
        return carry

    lax.fori_loop(0, NB, slot_step, 0)

    pl.semaphore_wait(barrier, len(others))
    mover = Mover(facing)
    send, arrived = mover.send, mover.arrived

    def own(other):
        return pl.ds(pl.multiple_of(other * ROWS, ROWS), ROWS)

    for d in (2, 1, 3):
        other = (g + d) % 4
        send(partial.at[own(other)], parts.at[d - 1], send_g.at[d - 1], recv_g.at[d - 1], member(other))
    total = partial[own(g), :]
    for d in (1, 3, 2):
        arrived(parts.at[d - 1], send_g.at[d - 1], recv_g.at[d - 1])
        total = total + parts[d - 1]
    solved = exact_dot(total, inverse_ref[...]).astype(BF16)
    a_ref[...] = solved
    full[x, 0, yh] = solved

    for d in offsets(NZ):
        send(
            full.at[x, 0, yh], full.at[x, slot_of(-d), yh],
            send_z.at[d - 1], recv_z.at[d - 1], device(x, (z + d) % NZ, y, c),
        )

    def first(k, start, size):
        for slot in range(start, start + size):
            for d in range(1, NZ):
                if slot_of(-d) == slot:
                    arrived(full.at[x, slot, yh], send_z.at[d - 1], recv_z.at[d - 1])
        here = full.at[x, pl.ds(start, size), yh]
        if k in X_FIRST_A:
            for d in offsets(NX):
                send(here, here, send_1.at[k, d - 1], recv_1.at[k, d - 1], device((x + d) % NX, z, y, c))
        else:
            send(here, here, send_1.at[k, 0], recv_1.at[k, 0], facing)

    def second(k, start, size):
        here = full.at[x, pl.ds(start, size), yh]
        if k in X_FIRST_A:
            for d in offsets(NX):
                arrived(here, send_1.at[k, d - 1], recv_1.at[k, d - 1])
            column = full.at[:, pl.ds(start, size), yh]
            send(column, column, send_2.at[k, 0], recv_2.at[k, 0], facing)
        else:
            arrived(here, send_1.at[k, 0], recv_1.at[k, 0])
            both = full.at[x, pl.ds(start, size)]
            for d in offsets(NX):
                send(both, both, send_2.at[k, d - 1], recv_2.at[k, d - 1], device((x + d) % NX, z, y, c))

    def third(k, start, size):
        if k in X_FIRST_A:
            arrived(full.at[:, pl.ds(start, size), yh], send_2.at[k, 0], recv_2.at[k, 0])
        else:
            for d in offsets(NX):
                arrived(full.at[x, pl.ds(start, size)], send_2.at[k, d - 1], recv_2.at[k, d - 1])

    order = groups()
    stages = (first, second, third)
    lags = (0, LAGS_A[0], LAGS_A[1])
    for t in range(len(order) + lags[-1]):
        for stage, lag in zip(stages, lags):
            if 0 <= t - lag < len(order):
                stage(t - lag, *order[t - lag])
    mover.finish()


def pick_kernel(fetch_ref, full, fetched_ref, units):
    z = place()[1]

    def pick(s, carry):
        f = fetch_ref[0, 0, s]
        owner, within = lax.div(f, 2), lax.rem(f, 2)
        start = pl.multiple_of(within * PIECE, PIECE)
        pair = lax.div(owner, YH)
        slot = slot_at(lax.rem(pair, NZ), z)
        unit = full[lax.div(pair, NZ), slot, lax.rem(owner, YH), pl.ds(start, PIECE), :]
        unit = unit.astype(F32)
        for h in range(2):
            units[h, pl.ds(pl.multiple_of(s * PIECE, PIECE), PIECE), :] = unit[:, h * 128:(h + 1) * 128]
        return carry

    lax.fori_loop(0, SLOTS, pick, 0, unroll=4)
    for r in range(PIECE):
        for h in range(2):
            at = r * R + h * 128
            picked = units.at[h][pl.ds(r, SLOTS, stride=PIECE), :]
            fetched_ref[0, 0, :, at:at + 128] = picked.astype(BF16)


def dma(*shape):
    return pltpu.SemaphoreType.DMA(shape)


VMEM = pl.BlockSpec(memory_space=pltpu.VMEM)
SMEM = pl.BlockSpec(memory_space=pltpu.SMEM)
ANY = pl.BlockSpec(memory_space=pl.ANY)


def on_device(values, counts, row_block, col_block, depth_block, factor_b, factor_c, fetch_list):
    n_groups = len(groups())
    full_b, own_c, cubes, system = pl.pallas_call(
        gather_kernel,
        out_shape=(
            jax.ShapeDtypeStruct((NX, NZ, NY, NC, PIECE, R), BF16),
            jax.ShapeDtypeStruct((R, R), BF16),
            jax.ShapeDtypeStruct((NB, EDGE, EDGE * EDGE), BF16),
            jax.ShapeDtypeStruct((R, R), F32),
        ),
        in_specs=[ANY] * 3,
        out_specs=(VMEM,) * 4,
        scratch_shapes=[
            pltpu.VMEM((4, R, R), BF16),
            dma(3), dma(NZ - 1), dma(NZ - 1), dma(n_groups, 3), dma(n_groups, 3),
            dma(n_groups, 3), dma(n_groups, 3), dma(n_groups), dma(n_groups), dma(3), dma(3),
        ],
        compiler_params=pltpu.CompilerParams(
            collective_id=0, has_side_effects=True, vmem_limit_bytes=24 << 20
        ),
        name="gather_factors",
    )(factor_b, factor_c, values)
    inverse, rows_b, rows_c, keep = pl.pallas_call(
        inverse_kernel,
        out_shape=(
            jax.ShapeDtypeStruct((R, R), F32),
            jax.ShapeDtypeStruct((NB, EDGE, R), F32),
            jax.ShapeDtypeStruct((NB, EDGE, R), BF16),
            jax.ShapeDtypeStruct((NB, 2, 8, R), jnp.int32),
        ),
        in_specs=[SMEM] * 4 + [VMEM] * 3,
        out_specs=(VMEM,) * 4,
        scratch_shapes=[pltpu.VMEM((R, R), F32)],
        compiler_params=pltpu.CompilerParams(vmem_limit_bytes=24 << 20),
        name="invert_select",
    )(counts, row_block, col_block, depth_block, full_b, own_c, system)
    a_new, full_a = pl.pallas_call(
        update_kernel,
        out_shape=(
            jax.ShapeDtypeStruct((ROWS, R), BF16),
            jax.ShapeDtypeStruct((NX, NZ, YH, ROWS, R), BF16),
        ),
        in_specs=[VMEM] * 5,
        out_specs=(VMEM, VMEM),
        scratch_shapes=[
            pltpu.VMEM((2 * EDGE, R), F32),
            pltpu.VMEM((4, R, R), BF16),
            pltpu.VMEM((3, ROWS, R), F32),
            dma(3), dma(3), dma(NZ - 1), dma(NZ - 1), dma(n_groups, 3), dma(n_groups, 3),
            dma(n_groups, 3), dma(n_groups, 3),
        ],
        compiler_params=pltpu.CompilerParams(
            collective_id=1, has_side_effects=True, vmem_limit_bytes=24 << 20
        ),
        name="update_gather",
    )(cubes, rows_b, rows_c, keep, inverse)
    fetched = pl.pallas_call(
        pick_kernel,
        out_shape=jax.ShapeDtypeStruct((1, 1, SLOTS, PIECE * R), BF16),
        in_specs=[SMEM, VMEM],
        out_specs=VMEM,
        scratch_shapes=[pltpu.VMEM((2, SLOTS * PIECE, 128), F32)],
        compiler_params=pltpu.CompilerParams(vmem_limit_bytes=16 << 20),
        name="pick_units",
    )(fetch_list, full_a)
    return a_new, fetched


def solution(mesh):
    placed = (
        P("blk", "grp", None, None, None),
        P("blk", "grp"),
        P("blk", "grp", None),
        P("blk", "grp", None),
        P("blk", "grp", None),
        P("blk", None),
        P("grp", None),
        P("blk", "grp", None),
    )
    return jax.shard_map(
        on_device,
        mesh=mesh,
        in_specs=placed,
        out_specs=(P(("blk", "grp"), None), P("blk", "grp", None, None)),
        check_vma=False,
    )
```

time: 182 us -> 113 us (0.62)
  the two profiles are of different devices: /device:TPU:40 before, /device:TPU:2 now
where the time goes in v2:
time: 113 us
  Pallas kernels  107 us (95%)
  local copies, waits for them, and re-layouts  4.17 us (4%)
  between operations  1.4 us (1%)
    pallas_call x1, Pallas kernels, on_device(): pl.pallas_call(gather_kernel, out_shape=(jax.ShapeDtypeStruct((NX, NZ, NY...  50.6 us
    pallas_call x1, Pallas kernels, on_device(): pl.pallas_call(update_kernel, out_shape=(jax.ShapeDtypeStruct((ROWS, R),...  47.2 us
    pallas_call x1, Pallas kernels, on_device(): pl.pallas_call(inverse_kernel, out_shape=(jax.ShapeDtypeStruct((R, R), F3...  6.47 us
    unnamed x15, local copies, waits for them, and re-layouts  4.17 us
    pallas_call x1, Pallas kernels, on_device(): pl.pallas_call(pick_kernel, out_shape=jax.ShapeDtypeStruct((1, 1, SLOTS,...  2.79 us

profile of v2, /device:TPU:2, one launch (start us, length us, event | category | flops | bytes accessed | tf_op | source)
XLA Modules:
  0.0 112.6 jit_solution(17747303845872444189)
XLA Ops:
  0.6 0.0 copy-start.5
  0.6 0.0 copy-start.4
  0.7 0.0 copy-start.3
  1.3 0.0 copy-start
  1.3 1.9 %copy-done = bf16[1,1,6,64,4096]{4,3,2,1,0:T(8,128)(2,1)S(1)} copy-done((bf16[1,1,6,64,4096]{4,3,2,1,0:T(8,128)(2,1)S(1)}, bf16[1,1,6,64,4096]{4,3,2,1,0:T(8,128)(2,1)}, u32[]{:S(2)}) %copy-start) | copy-done | bytes 3145752
  3.2 0.0 copy-start.1
  3.2 0.9 copy-done.1
  4.1 0.0 copy-start.2
  4.1 0.8 copy-done.2
  4.9 50.6 %gather_factors.1 = (bf16[4,16,4,2,16,256]{5,4,3,2,1,0:T(8,128)(2,1)S(1)}, bf16[256,256]{1,0:T(8,128)(2,1)S(1)}, bf16[6,64,4096]{2,1,0:T(8,128)(2,1)S(1)}, f32[256,256]{1,0:T(8,128)S(1)}) custom-call(bf16[64,256]{1,0:T(8,128)(2,1)S(1)} %copy-done.2, bf16[256,256]{1,0:T(8,128)(2,1)S(1)} %copy-done.1, bf16[1,1,6,64,4096]{4,3,2,1,0:T(8,128)(2,1)S(1)} %copy-done), custom_call_target="tpu_custom_call" | custom-call | tf_op jit(solution)/shard_map/gather_factors/pallas_call | solution.py:428
  55.5 0.0 copy-done.5
  55.5 0.0 copy-done.4
  55.5 0.0 copy-done.3
  55.5 6.5 %invert_select.1 = (f32[256,256]{1,0:T(8,128)S(1)}, f32[6,64,256]{2,1,0:T(8,128)S(1)}, bf16[6,64,256]{2,1,0:T(8,128)(2,1)S(1)}, s32[6,2,8,256]{3,2,1,0:T(8,128)S(1)}) custom-call(s32[1,1]{1,0:T(1,128)S(6)} %copy.11.counts_ref, s32[1,1,6]{2,1,0:T(1,128)S(1)} %copy-done.3, s32[1,1,6]{2,1,0:T(1,128)S(1)} %copy-done.4, s32[1,1,6]{2,1,0:T(1,128)S(1)} %copy-done.5, ...), custom_call_target="tpu_custom_call" | custom-call | tf_op jit(solution)/shard_map/invert_select/pallas_call | solution.py:448
  62.0 0.0 copy-start.6
  62.0 47.2 %update_gather.1 = (bf16[32,256]{1,0:T(8,128)(2,1)S(1)}, bf16[4,16,2,32,256]{4,3,2,1,0:T(8,128)(2,1)S(1)}) custom-call(bf16[6,64,4096]{2,1,0:T(8,128)(2,1)S(1)} %get-tuple-element.12.cubes, f32[6,64,256]{2,1,0:T(8,128)S(1)} %get-tuple-element.16.rows_b_ref, bf16[6,64,256]{2,1,0:T(8,128)(2,1)S(1)} %get-tuple-element.17.rows_c_ref, ...), custom_call_target="tpu_custom_call" | custom-call | tf_op jit(solution)/shard_map/update_gather/pallas_call | solution.py:462
  109.2 0.0 copy-done.6
  109.2 2.8 %pick_units.1 = bf16[1,1,64,4096]{3,2,1,0:T(8,128)(2,1)} custom-call(s32[1,1,64]{2,1,0:T(1,128)S(1)} %copy-done.6, bf16[4,16,2,32,256]{4,3,2,1,0:T(8,128)(2,1)S(1)} %get-tuple-element.21.full), custom_call_target="tpu_custom_call" | custom-call | tf_op jit(solution)/shard_map/pick_units/pallas_call | solution.py:482
  112.0 0.6 copy.12
Async XLA Ops:
  0.6 54.8 %copy-start.5 = (s32[1,1,6]{2,1,0:T(1,128)S(1)}, s32[1,1,6]{2,1,0:T(1,128)}, u32[]{:S(2)}) copy-start(s32[1,1,6]{2,1,0:T(1,128)} %depth_ref.1) | copy-start | bytes 76
  0.6 54.8 %copy-start.4 = (s32[1,1,6]{2,1,0:T(1,128)S(1)}, s32[1,1,6]{2,1,0:T(1,128)}, u32[]{:S(2)}) copy-start(s32[1,1,6]{2,1,0:T(1,128)} %col_ref.1) | copy-start | bytes 76
  0.7 54.8 %copy-start.3 = (s32[1,1,6]{2,1,0:T(1,128)S(1)}, s32[1,1,6]{2,1,0:T(1,128)}, u32[]{:S(2)}) copy-start(s32[1,1,6]{2,1,0:T(1,128)} %row_ref.1) | copy-start | bytes 76
  1.3 1.9 %copy-start = (bf16[1,1,6,64,4096]{4,3,2,1,0:T(8,128)(2,1)S(1)}, bf16[1,1,6,64,4096]{4,3,2,1,0:T(8,128)(2,1)}, u32[]{:S(2)}) copy-start(bf16[1,1,6,64,4096]{4,3,2,1,0:T(8,128)(2,1)} %values_ref.1) | copy-start | bytes 9437188
  3.2 0.9 copy-start.1
  4.1 0.8 copy-start.2
  62.0 47.2 %copy-start.6 = (s32[1,1,64]{2,1,0:T(1,128)S(1)}, s32[1,1,64]{2,1,0:T(1,128)}, u32[]{:S(2)}) copy-start(s32[1,1,64]{2,1,0:T(1,128)} %fetch_ref.1) | copy-start | bytes 772

commit v3 on v2

--- a/solution.py
+++ b/solution.py
@@ -30,21 +30,22 @@
     return ((x * NZ + z) * YH + y // 2, (y % 2) * NC + c)
 
 
-def greet(others):
+def announce(others):
     barrier = pltpu.get_barrier_semaphore()
     for other in others:
         pl.semaphore_signal(barrier, inc=1, device_id=other, device_id_type=MESH)
-    pl.semaphore_wait(barrier, len(others))
-
-
-def slot_of(d):
-    d = d % NZ
-    return max(2 * d - 1, 0) if d <= NZ // 2 else 2 * (NZ - d)
+
+
+def await_greetings(others):
+    pl.semaphore_wait(pltpu.get_barrier_semaphore(), len(others))
 
 
 def slot_at(z_there, z_here):
-    d = lax.rem(z_there - z_here + NZ, NZ)
-    return jnp.where(d <= NZ // 2, jnp.maximum(2 * d - 1, 0), 2 * (NZ - d))
+    d = lax.rem(z_here - z_there + NZ, NZ)
+    left = d <= NZ // 2
+    step = jnp.where(left, d, NZ - d) - 1
+    slot = 4 * (step // 2) + step % 2 + jnp.where(left, 1, 3)
+    return jnp.where(d == 0, 0, slot)
 
 
 def groups():
@@ -60,6 +61,15 @@
     return order
 
 
+def schedule(gaps):
+    events = []
+    for k in range(len(groups())):
+        time = (k + 1) // 2 * 2.2
+        for stage in range(len(gaps) + 1):
+            events.append((time + sum(gaps[:stage]), stage, k))
+    return [event[1:] for event in sorted(events)]
+
+
 class Mover:
     def __init__(self, other):
         self.sent, self.other = [], other
@@ -83,52 +93,80 @@
             copy.wait_send()
 
 
-LAGS_B = (1, 2, 3)
-LAGS_A = (1, 2)
+class Chain:
+    def __init__(self, mover, at, send_sem, recv_sem, x, z, y, c):
+        self.mover, self.at, self.send_sem, self.recv_sem = mover, at, send_sem, recv_sem
+        self.place = x, z, y, c
+
+    def peer(self, d):
+        x, z, y, c = self.place
+        return device(x, (z + d + NZ) % NZ, y, c)
+
+    def start(self):
+        for i, d in enumerate((1, 2, -1, -2)):
+            self.mover.send(
+                self.at(0, 1), self.at(1 + i, 1), self.send_sem.at[i], self.recv_sem.at[i], self.peer(d)
+            )
+
+    def arrive(self, k):
+        order = groups()
+        if k in (1, 2):
+            for i in (2 * k - 2, 2 * k - 1):
+                self.mover.arrived(self.at(1 + i, 1), self.send_sem.at[i], self.recv_sem.at[i])
+        elif k > 2:
+            self.mover.arrived(self.at(*order[k]), self.send_sem.at[k + 1], self.recv_sem.at[k + 1])
+        if 1 <= k < len(order) - 2:
+            start, size = order[k + 2]
+            self.mover.send(
+                self.at(order[k][0], size), self.at(start, size),
+                self.send_sem.at[k + 3], self.recv_sem.at[k + 3], self.peer(2 if k % 2 else -2),
+            )
+
+
+GAPS_B = (2.3, 4.5, 2.2)
+GAPS_A = (2.3, 4.5)
 X_FIRST_B = (1, 3, 5, 7)
 X_FIRST_A = (1, 2, 4, 5, 7)
 
 
 def gather_kernel(
-    b_ref, c_ref, values_ref,
-    full, own_c, cubes, system_ref,
+    b_ref, c_ref,
+    full, own_c, system_ref,
     full_c,
     local_sem, send_z, recv_z, send_1, recv_1, send_2, recv_2, send_s, recv_s, send_c, recv_c,
 ):
     x, z, y, c = place()
     g = (y % 2) * NC + c
     sibling = device(x, z, y, 1 - c)
-    across = device(x, z, y + 1 - 2 * (y % 2), c)
+    g_across = g + 2 - 4 * (y % 2)
+
+    def c_half(i):
+        return pl.ds(i * R // 2, R // 2)
+
     own_rows = pl.ds(pl.multiple_of(g * PIECE, PIECE), PIECE)
     loads = [
         pltpu.make_async_copy(b_ref.at[own_rows], full.at[x, 0, y, c], local_sem.at[0]),
         pltpu.make_async_copy(c_ref, own_c, local_sem.at[1]),
-        pltpu.make_async_copy(values_ref.at[0, 0], cubes, local_sem.at[2]),
     ]
     for load in loads:
         load.start()
 
-    others = [device(x, (z + d) % NZ, y, c) for d in range(1, NZ)]
+    others = [device(x, (z + d + NZ) % NZ, y, c) for d in (1, 2, -1, -2)]
     others += [device((x + d) % NX, z, y, c) for d in range(1, NX)]
     others += [device(x, z, (y + d) % NY, c) for d in range(1, NY)]
     others += [sibling]
+    announce(others)
     loads[0].wait()
     loads[1].wait()
-    greet(others)
+    await_greetings(others)
     mover = Mover(sibling)
+    chain = Chain(mover, lambda i, n: full.at[x, pl.ds(i, n), y, c], send_z, recv_z, x, z, y, c)
     send, arrived = mover.send, mover.arrived
 
-    for d in offsets(NZ):
-        send(
-            full.at[x, 0, y, c], full.at[x, slot_of(-d), y, c],
-            send_z.at[d - 1], recv_z.at[d - 1], device(x, (z + d) % NZ, y, c),
-        )
+    chain.start()
 
     def first(k, start, size):
-        for slot in range(start, start + size):
-            for d in range(1, NZ):
-                if slot_of(-d) == slot:
-                    arrived(full.at[x, slot, y, c], send_z.at[d - 1], recv_z.at[d - 1])
+        chain.arrive(k)
         here = full.at[x, pl.ds(start, size), y, c]
         for d in offsets(4):
             there = device((x + d) % NX, z, y, c) if k in X_FIRST_B else device(x, z, (y + d) % NY, c)
@@ -166,25 +204,23 @@
 
     parts = groups()
     stages = (first, second, third, fourth)
-    lags = (0,) + LAGS_B
-    for t in range(len(parts) + lags[-1]):
-        for stage, lag in zip(stages, lags):
-            if 0 <= t - lag < len(parts):
-                stage(t - lag, *parts[t - lag])
-        if t == 0:
-            send(own_c, full_c.at[g], send_c.at[0], recv_c.at[0], across)
-            send(own_c, full_c.at[g], send_c.at[1], recv_c.at[1], sibling)
-            g_across = g + 2 - 4 * (y % 2)
+    for stage, k in schedule(GAPS_B):
+        stages[stage](k, *parts[k])
+        if (stage, k) == (0, 0):
+            for i, d in enumerate((1, NY - 1)):
+                there = device(x, z, (y + d) % NY, c)
+                send(own_c.at[c_half(i)], full_c.at[g, c_half(i)], send_c.at[i], recv_c.at[i], there)
+            send(own_c, full_c.at[g], send_c.at[2], recv_c.at[2], sibling)
             gram_c = gram(own_c[...])
-        if t == 3:
-            arrived(full_c.at[g_across], send_c.at[0], recv_c.at[0])
-            send(full_c.at[g_across], full_c.at[g_across], send_c.at[2], recv_c.at[2], sibling)
+        if (stage, k) == (1, 2):
+            for i in range(2):
+                arrived(full_c.at[g_across, c_half(i)], send_c.at[i], recv_c.at[i])
+            send(full_c.at[g_across], full_c.at[g_across], send_c.at[3], recv_c.at[3], sibling)
             gram_c = gram_c + gram(full_c[g_across])
-    for i, other in ((1, g + 1 - 2 * c), (2, g_across + 1 - 2 * c)):
+    for i, other in ((2, g + 1 - 2 * c), (3, g_across + 1 - 2 * c)):
         arrived(full_c.at[other], send_c.at[i], recv_c.at[i])
         gram_c = gram_c + gram(full_c[other])
     system_ref[...] = grams[0] * gram_c
-    loads[2].wait()
     mover.finish()
 
 
@@ -280,7 +316,7 @@
 
 
 def update_kernel(
-    cubes, rows_b_ref, rows_c_ref, keep_ref, inverse_ref,
+    values_ref, rows_b_ref, rows_c_ref, keep_ref, inverse_ref,
     a_ref, full,
     partial, weights, parts,
     send_g, recv_g, send_z, recv_z, send_1, recv_1, send_2, recv_2,
@@ -294,12 +330,10 @@
         return device(x, z, yh * 2 + other // NC, other % NC)
 
     others = [member((g + d) % 4) for d in range(1, 4)]
-    others += [device(x, (z + d) % NZ, y, c) for d in range(1, NZ)]
+    others += [device(x, (z + d + NZ) % NZ, y, c) for d in (1, 2, -1, -2)]
     others += [device((x + d) % NX, z, y, c) for d in range(1, NX)]
     others += [facing]
-    barrier = pltpu.get_barrier_semaphore()
-    for other in others:
-        pl.semaphore_signal(barrier, inc=1, device_id=other, device_id_type=MESH)
+    announce(others)
 
     partial[...] = jnp.zeros_like(partial)
     weights[...] = jnp.zeros_like(weights)
@@ -310,7 +344,7 @@
             weights[q, q * EDGE:(q + 1) * EDGE, :] = rows_c_ref[s]
         b_rows = rows_b_ref[s]
         cube = jnp.concatenate(
-            [cubes[s, :, t * R:(t + 1) * R] for t in range(chunks)], axis=0
+            [values_ref[0, 0, s, :, t * R:(t + 1) * R] for t in range(chunks)], axis=0
         )
         term = jnp.zeros((EDGE, R), F32)
         for q in range(4):
@@ -325,8 +359,9 @@
 
     lax.fori_loop(0, NB, slot_step, 0)
 
-    pl.semaphore_wait(barrier, len(others))
+    await_greetings(others)
     mover = Mover(facing)
+    chain = Chain(mover, lambda i, n: full.at[x, pl.ds(i, n), yh], send_z, recv_z, x, z, y, c)
     send, arrived = mover.send, mover.arrived
 
     def own(other):
@@ -343,17 +378,10 @@
     a_ref[...] = solved
     full[x, 0, yh] = solved
 
-    for d in offsets(NZ):
-        send(
-            full.at[x, 0, yh], full.at[x, slot_of(-d), yh],
-            send_z.at[d - 1], recv_z.at[d - 1], device(x, (z + d) % NZ, y, c),
-        )
+    chain.start()
 
     def first(k, start, size):
-        for slot in range(start, start + size):
-            for d in range(1, NZ):
-                if slot_of(-d) == slot:
-                    arrived(full.at[x, slot, yh], send_z.at[d - 1], recv_z.at[d - 1])
+        chain.arrive(k)
         here = full.at[x, pl.ds(start, size), yh]
         if k in X_FIRST_A:
             for d in offsets(NX):
@@ -383,15 +411,13 @@
 
     order = groups()
     stages = (first, second, third)
-    lags = (0, LAGS_A[0], LAGS_A[1])
-    for t in range(len(order) + lags[-1]):
-        for stage, lag in zip(stages, lags):
-            if 0 <= t - lag < len(order):
-                stage(t - lag, *order[t - lag])
+    for stage, k in schedule(GAPS_A):
+        stages[stage](k, *order[k])
     mover.finish()
 
 
-def pick_kernel(fetch_ref, full, fetched_ref, units):
+def pick_kernel(fetch_ref, solved_ref, full, a_ref, fetched_ref, units):
+    a_ref[...] = solved_ref[...]
     z = place()[1]
 
     def pick(s, carry):
@@ -406,7 +432,7 @@
             units[h, pl.ds(pl.multiple_of(s * PIECE, PIECE), PIECE), :] = unit[:, h * 128:(h + 1) * 128]
         return carry
 
-    lax.fori_loop(0, SLOTS, pick, 0, unroll=4)
+    lax.fori_loop(0, SLOTS, pick, 0, unroll=16)
     for r in range(PIECE):
         for h in range(2):
             at = r * R + h * 128
@@ -420,31 +446,30 @@
 
 VMEM = pl.BlockSpec(memory_space=pltpu.VMEM)
 SMEM = pl.BlockSpec(memory_space=pltpu.SMEM)
-ANY = pl.BlockSpec(memory_space=pl.ANY)
+HBM = pl.BlockSpec(memory_space=pltpu.HBM)
 
 
 def on_device(values, counts, row_block, col_block, depth_block, factor_b, factor_c, fetch_list):
     n_groups = len(groups())
-    full_b, own_c, cubes, system = pl.pallas_call(
+    full_b, own_c, system = pl.pallas_call(
         gather_kernel,
         out_shape=(
             jax.ShapeDtypeStruct((NX, NZ, NY, NC, PIECE, R), BF16),
             jax.ShapeDtypeStruct((R, R), BF16),
-            jax.ShapeDtypeStruct((NB, EDGE, EDGE * EDGE), BF16),
             jax.ShapeDtypeStruct((R, R), F32),
         ),
-        in_specs=[ANY] * 3,
-        out_specs=(VMEM,) * 4,
+        in_specs=[HBM] * 2,
+        out_specs=(VMEM,) * 3,
         scratch_shapes=[
             pltpu.VMEM((4, R, R), BF16),
-            dma(3), dma(NZ - 1), dma(NZ - 1), dma(n_groups, 3), dma(n_groups, 3),
-            dma(n_groups, 3), dma(n_groups, 3), dma(n_groups), dma(n_groups), dma(3), dma(3),
+            dma(2), dma(n_groups + 1), dma(n_groups + 1), dma(n_groups, 3), dma(n_groups, 3),
+            dma(n_groups, 3), dma(n_groups, 3), dma(n_groups), dma(n_groups), dma(4), dma(4),
         ],
         compiler_params=pltpu.CompilerParams(
             collective_id=0, has_side_effects=True, vmem_limit_bytes=24 << 20
         ),
         name="gather_factors",
-    )(factor_b, factor_c, values)
+    )(factor_b, factor_c)
     inverse, rows_b, rows_c, keep = pl.pallas_call(
         inverse_kernel,
         out_shape=(
@@ -459,7 +484,7 @@
         compiler_params=pltpu.CompilerParams(vmem_limit_bytes=24 << 20),
         name="invert_select",
     )(counts, row_block, col_block, depth_block, full_b, own_c, system)
-    a_new, full_a = pl.pallas_call(
+    solved, full_a = pl.pallas_call(
         update_kernel,
         out_shape=(
             jax.ShapeDtypeStruct((ROWS, R), BF16),
@@ -471,24 +496,26 @@
             pltpu.VMEM((2 * EDGE, R), F32),
             pltpu.VMEM((4, R, R), BF16),
             pltpu.VMEM((3, ROWS, R), F32),
-            dma(3), dma(3), dma(NZ - 1), dma(NZ - 1), dma(n_groups, 3), dma(n_groups, 3),
+            dma(3), dma(3), dma(n_groups + 1), dma(n_groups + 1), dma(n_groups, 3), dma(n_groups, 3),
             dma(n_groups, 3), dma(n_groups, 3),
         ],
         compiler_params=pltpu.CompilerParams(
             collective_id=1, has_side_effects=True, vmem_limit_bytes=24 << 20
         ),
         name="update_gather",
-    )(cubes, rows_b, rows_c, keep, inverse)
-    fetched = pl.pallas_call(
+    )(values, rows_b, rows_c, keep, inverse)
+    return pl.pallas_call(
         pick_kernel,
-        out_shape=jax.ShapeDtypeStruct((1, 1, SLOTS, PIECE * R), BF16),
-        in_specs=[SMEM, VMEM],
-        out_specs=VMEM,
+        out_shape=(
+            jax.ShapeDtypeStruct((ROWS, R), BF16),
+            jax.ShapeDtypeStruct((1, 1, SLOTS, PIECE * R), BF16),
+        ),
+        in_specs=[SMEM, VMEM, VMEM],
+        out_specs=(VMEM, VMEM),
         scratch_shapes=[pltpu.VMEM((2, SLOTS * PIECE, 128), F32)],
         compiler_params=pltpu.CompilerParams(vmem_limit_bytes=16 << 20),
         name="pick_units",
-    )(fetch_list, full_a)
-    return a_new, fetched
+    )(fetch_list, solved, full_a)
 
 
 def solution(mesh):

time: 113 us -> 90.9 us (0.80)
  the two profiles are of different devices: /device:TPU:2 before, /device:TPU:32 now
where the time goes in v3:
time: 90.9 us; the launch traced here: 90.7 us
  Pallas kernels  85.4 us (94%)
  local copies, waits for them, and re-layouts  3.78 us (4%)
  between operations  1.5 us (2%)
    pallas_call x1, Pallas kernels, on_device(): pl.pallas_call(gather_kernel, out_shape=(jax.ShapeDtypeStruct((NX, NZ, NY...  39 us
    pallas_call x1, Pallas kernels, on_device(): pl.pallas_call(update_kernel, out_shape=(jax.ShapeDtypeStruct((ROWS, R),...  36.9 us
    pallas_call x1, Pallas kernels, on_device(): pl.pallas_call(inverse_kernel, out_shape=(jax.ShapeDtypeStruct((R, R), F3...  6.46 us
    unnamed x14, local copies, waits for them, and re-layouts  3.78 us
    pallas_call x1, Pallas kernels, on_device(): pl.pallas_call(pick_kernel, out_shape=(jax.ShapeDtypeStruct((ROWS, R), BF...  3.1 us

profile of v3, /device:TPU:32, one launch (start us, length us, event | category | flops | bytes accessed | tf_op | source)
XLA Modules:
  0.0 90.7 jit_solution(12498488147626123318)
XLA Ops:
  0.6 0.0 copy-start
  1.4 0.0 copy-start.1
  1.4 1.1 %copy-done.1 = bf16[256,256]{1,0:T(8,128)(2,1)S(1)} copy-done((bf16[256,256]{1,0:T(8,128)(2,1)S(1)}, bf16[256,256]{1,0:T(8,128)(2,1)}, u32[]{:S(2)}) %copy-start.1) | copy-done | bytes 131096
  2.5 0.0 copy-start.2
  2.5 0.8 copy-done.2
  3.3 39.0 %gather_factors.1 = (bf16[4,16,4,2,16,256]{5,4,3,2,1,0:T(8,128)(2,1)S(1)}, bf16[256,256]{1,0:T(8,128)(2,1)S(1)}, f32[256,256]{1,0:T(8,128)S(1)}) custom-call(bf16[64,256]{1,0:T(8,128)(2,1)S(1)} %copy-done.2, bf16[256,256]{1,0:T(8,128)(2,1)S(1)} %copy-done.1), custom_call_target="tpu_custom_call" | custom-call | tf_op jit(solution)/shard_map/gather_factors/pallas_call | solution.py:454
  42.2 0.0 copy-start.3
  42.2 0.6 copy-done.3
  42.9 0.0 copy-start.4
  42.9 0.7 copy-done.4
  43.5 0.0 copy-start.5
  43.5 0.7 copy-done.5
  44.2 6.5 %invert_select.1 = (f32[256,256]{1,0:T(8,128)S(1)}, f32[6,64,256]{2,1,0:T(8,128)S(1)}, bf16[6,64,256]{2,1,0:T(8,128)(2,1)S(1)}, s32[6,2,8,256]{3,2,1,0:T(8,128)S(1)}) custom-call(s32[1,1]{1,0:T(1,128)S(6)} %copy.10.counts_ref, s32[1,1,6]{2,1,0:T(1,128)S(1)} %copy-done.3, s32[1,1,6]{2,1,0:T(1,128)S(1)} %copy-done.4, s32[1,1,6]{2,1,0:T(1,128)S(1)} %copy-done.5, ...), custom_call_target="tpu_custom_call" | custom-call | tf_op jit(solution)/shard_map/invert_select/pallas_call | solution.py:473
  50.7 0.0 copy-start.6
  50.7 0.0 copy-done
  50.7 36.9 %update_gather.1 = (bf16[32,256]{1,0:T(8,128)(2,1)S(1)}, bf16[4,16,2,32,256]{4,3,2,1,0:T(8,128)(2,1)S(1)}) custom-call(bf16[1,1,6,64,4096]{4,3,2,1,0:T(8,128)(2,1)S(1)} %copy-done, f32[6,64,256]{2,1,0:T(8,128)S(1)} %get-tuple-element.14.rows_b_ref, bf16[6,64,256]{2,1,0:T(8,128)(2,1)S(1)} %get-tuple-element.15.rows_c_ref, ...), custom_call_target="tpu_custom_call" | custom-call | tf_op jit(solution)/shard_map/update_gather/pallas_call | solution.py:487
  87.6 0.0 copy-done.6
  87.6 3.1 %pick_units.1 = (bf16[32,256]{1,0:T(8,128)(2,1)}, bf16[1,1,64,4096]{3,2,1,0:T(8,128)(2,1)}) custom-call(s32[1,1,64]{2,1,0:T(1,128)S(1)} %copy-done.6, bf16[32,256]{1,0:T(8,128)(2,1)S(1)} %get-tuple-element.18.solved_ref, bf16[4,16,2,32,256]{4,3,2,1,0:T(8,128)(2,1)S(1)} %get-tuple-element.19.full), custom_call_target="tpu_custom_call" | custom-call | tf_op jit(solution)/shard_map/pick_units/pallas_call | solution.py:507
Async XLA Ops:
  0.6 50.0 %copy-start = (bf16[1,1,6,64,4096]{4,3,2,1,0:T(8,128)(2,1)S(1)}, bf16[1,1,6,64,4096]{4,3,2,1,0:T(8,128)(2,1)}, u32[]{:S(2)}) copy-start(bf16[1,1,6,64,4096]{4,3,2,1,0:T(8,128)(2,1)} %values_ref.1) | copy-start | bytes 9437188
  1.4 1.1 %copy-start.1 = (bf16[256,256]{1,0:T(8,128)(2,1)S(1)}, bf16[256,256]{1,0:T(8,128)(2,1)}, u32[]{:S(2)}) copy-start(bf16[256,256]{1,0:T(8,128)(2,1)} %c_ref.1) | copy-start | bytes 393220
  2.5 0.8 copy-start.2
  42.2 0.7 copy-start.3
  42.9 0.7 copy-start.4
  43.5 0.7 copy-start.5
  50.7 36.9 %copy-start.6 = (s32[1,1,64]{2,1,0:T(1,128)S(1)}, s32[1,1,64]{2,1,0:T(1,128)}, u32[]{:S(2)}) copy-start(s32[1,1,64]{2,1,0:T(1,128)} %fetch_ref.1) | copy-start | bytes 772

commit v4 on v3

--- a/solution.py
+++ b/solution.py
@@ -125,8 +125,8 @@
 
 GAPS_B = (2.3, 4.5, 2.2)
 GAPS_A = (2.3, 4.5)
-X_FIRST_B = (1, 3, 5, 7)
-X_FIRST_A = (1, 2, 4, 5, 7)
+X_FIRST_B = (0, 2, 4, 6, 8)
+X_FIRST_A = (0, 2, 3, 5, 6, 8)
 
 
 def gather_kernel(
@@ -296,9 +296,20 @@
 
 
 def inverse_kernel(
-    counts_ref, row_ref, col_ref, depth_ref, full_ref, c_ref, system_ref,
-    inverse_ref, rows_b_ref, rows_c_ref, keep_ref, work,
+    counts_ref, row_hbm, col_hbm, depth_hbm, full_ref, c_ref, system_ref,
+    inverse_ref, rows_b_ref, rows_c_ref, keep_ref, work, row_ref, col_ref, depth_ref, load_sem,
 ):
+    loads = [
+        pltpu.make_async_copy(source, target, load_sem.at[i])
+        for i, (source, target) in enumerate(
+            ((row_hbm, row_ref), (col_hbm, col_ref), (depth_hbm, depth_ref))
+        )
+    ]
+    for load in loads:
+        load.start()
+    invert(system_ref[...], inverse_ref, work)
+    for load in loads:
+        load.wait()
     z = place()[1]
     live = counts_ref[0, 0]
     for s in range(NB):
@@ -312,7 +323,6 @@
         for i in range(2):
             keep = jnp.logical_and(s < live, row_ref[0, 0, s] == i)
             keep_ref[s, i] = jnp.full((8, R), jnp.where(keep, 1, 0), jnp.int32)
-    invert(system_ref[...], inverse_ref, work)
 
 
 def update_kernel(
@@ -447,6 +457,10 @@
 VMEM = pl.BlockSpec(memory_space=pltpu.VMEM)
 SMEM = pl.BlockSpec(memory_space=pltpu.SMEM)
 HBM = pl.BlockSpec(memory_space=pltpu.HBM)
+
+
+def in_hbm(x):
+    return pltpu.with_memory_space_constraint(x, pltpu.HBM)
 
 
 def on_device(values, counts, row_block, col_block, depth_block, factor_b, factor_c, fetch_list):
@@ -469,7 +483,7 @@
             collective_id=0, has_side_effects=True, vmem_limit_bytes=24 << 20
         ),
         name="gather_factors",
-    )(factor_b, factor_c)
+    )(in_hbm(factor_b), in_hbm(factor_c))
     inverse, rows_b, rows_c, keep = pl.pallas_call(
         inverse_kernel,
         out_shape=(
@@ -478,12 +492,12 @@
             jax.ShapeDtypeStruct((NB, EDGE, R), BF16),
             jax.ShapeDtypeStruct((NB, 2, 8, R), jnp.int32),
         ),
-        in_specs=[SMEM] * 4 + [VMEM] * 3,
+        in_specs=[SMEM] + [HBM] * 3 + [VMEM] * 3,
         out_specs=(VMEM,) * 4,
-        scratch_shapes=[pltpu.VMEM((R, R), F32)],
+        scratch_shapes=[pltpu.VMEM((R, R), F32)] + [pltpu.SMEM((1, 1, NB), jnp.int32)] * 3 + [dma(3)],
         compiler_params=pltpu.CompilerParams(vmem_limit_bytes=24 << 20),
         name="invert_select",
-    )(counts, row_block, col_block, depth_block, full_b, own_c, system)
+    )(counts, in_hbm(row_block), in_hbm(col_block), in_hbm(depth_block), full_b, own_c, system)
     solved, full_a = pl.pallas_call(
         update_kernel,
         out_shape=(

time: 90.9 us -> 86.1 us (0.947)
  the two profiles are of different devices: /device:TPU:32 before, /device:TPU:2 now
where the time goes in v4:
time: 86.1 us; the launch traced here: 86 us
  Pallas kernels  84.5 us (98%)
  between operations  1.48 us (2%)
    pallas_call x1, Pallas kernels, on_device(): pl.pallas_call(gather_kernel, out_shape=(jax.ShapeDtypeStruct((NX, NZ, NY...  39.2 us
    pallas_call x1, Pallas kernels, on_device(): pl.pallas_call(update_kernel, out_shape=(jax.ShapeDtypeStruct((ROWS, R),...  36 us
    pallas_call x1, Pallas kernels, on_device(): pl.pallas_call(inverse_kernel, out_shape=(jax.ShapeDtypeStruct((R, R), F3...  6.11 us
    pallas_call x1, Pallas kernels, on_device(): pl.pallas_call(pick_kernel, out_shape=(jax.ShapeDtypeStruct((ROWS, R), BF...  3.1 us

profile of v4, /device:TPU:2, one launch (start us, length us, event | category | flops | bytes accessed | tf_op | source)
XLA Modules:
  0.0 86.0 jit_solution(9472846788370572839)
XLA Ops:
  0.6 0.0 copy-start
  1.4 39.2 %gather_factors.1 = (bf16[4,16,4,2,16,256]{5,4,3,2,1,0:T(8,128)(2,1)S(1)}, bf16[256,256]{1,0:T(8,128)(2,1)S(1)}, f32[256,256]{1,0:T(8,128)S(1)}) custom-call(bf16[64,256]{1,0:T(8,128)(2,1)} %b_ref.1, bf16[256,256]{1,0:T(8,128)(2,1)} %c_ref.1), custom_call_target="tpu_custom_call" | custom-call | tf_op jit(solution)/shard_map/gather_factors/pallas_call | solution.py:468
  40.7 6.1 %invert_select.1 = (f32[256,256]{1,0:T(8,128)S(1)}, f32[6,64,256]{2,1,0:T(8,128)S(1)}, bf16[6,64,256]{2,1,0:T(8,128)(2,1)S(1)}, s32[6,2,8,256]{3,2,1,0:T(8,128)S(1)}) custom-call(s32[1,1]{1,0:T(1,128)S(6)} %copy.10.counts_ref, s32[1,1,6]{2,1,0:T(1,128)} %row_hbm.1, s32[1,1,6]{2,1,0:T(1,128)} %col_hbm.1, s32[1,1,6]{2,1,0:T(1,128)} %depth_hbm.1, ...), custom_call_target="tpu_custom_call" | custom-call | tf_op jit(solution)/shard_map/invert_select/pallas_call | solution.py:487
  46.8 0.0 copy-start.1
  46.8 0.0 copy-done
  46.8 36.0 %update_gather.1 = (bf16[32,256]{1,0:T(8,128)(2,1)S(1)}, bf16[4,16,2,32,256]{4,3,2,1,0:T(8,128)(2,1)S(1)}) custom-call(bf16[1,1,6,64,4096]{4,3,2,1,0:T(8,128)(2,1)S(1)} %copy-done, f32[6,64,256]{2,1,0:T(8,128)S(1)} %get-tuple-element.14.rows_b_ref, bf16[6,64,256]{2,1,0:T(8,128)(2,1)S(1)} %get-tuple-element.15.rows_c_ref, ...), custom_call_target="tpu_custom_call" | custom-call | tf_op jit(solution)/shard_map/update_gather/pallas_call | solution.py:501
  82.8 0.0 copy-done.1
  82.9 3.1 %pick_units.1 = (bf16[32,256]{1,0:T(8,128)(2,1)}, bf16[1,1,64,4096]{3,2,1,0:T(8,128)(2,1)}) custom-call(s32[1,1,64]{2,1,0:T(1,128)S(1)} %copy-done.1, bf16[32,256]{1,0:T(8,128)(2,1)S(1)} %get-tuple-element.18.solved_ref, bf16[4,16,2,32,256]{4,3,2,1,0:T(8,128)(2,1)S(1)} %get-tuple-element.19.full), custom_call_target="tpu_custom_call" | custom-call | tf_op jit(solution)/shard_map/pick_units/pallas_call | solution.py:521
Async XLA Ops:
  0.6 46.2 %copy-start = (bf16[1,1,6,64,4096]{4,3,2,1,0:T(8,128)(2,1)S(1)}, bf16[1,1,6,64,4096]{4,3,2,1,0:T(8,128)(2,1)}, u32[]{:S(2)}) copy-start(bf16[1,1,6,64,4096]{4,3,2,1,0:T(8,128)(2,1)} %values_ref.1) | copy-start | bytes 9437188
  46.8 36.0 %copy-start.1 = (s32[1,1,64]{2,1,0:T(1,128)S(1)}, s32[1,1,64]{2,1,0:T(1,128)}, u32[]{:S(2)}) copy-start(s32[1,1,64]{2,1,0:T(1,128)} %fetch_ref.1) | copy-start | bytes 772

commit v5 on v4

--- a/solution.py
+++ b/solution.py
@@ -255,10 +255,12 @@
     start = 1.0 / bound
     rest = eye - scaled * start
     guess = (eye + rest) * start
-    for _ in range(7):
-        rest_parts = split(rest)
-        rest = three_pass(rest_parts, rest_parts)
-        guess = guess + three_pass(split(rest), split(guess))
+    rest_parts = split(rest)
+    rest = three_pass(rest_parts, rest_parts)
+    for _ in range(6):
+        both = three_pass(split(rest), split(jnp.concatenate([rest, guess], axis=1)))
+        rest, guess = both[:, :R], guess + both[:, R:]
+    guess = guess + three_pass(split(rest), split(guess))
     work[...] = guess
 
     def unfinished(state):

time: 86.1 us -> 86.1 us (level)
  no operation moved by 1% of the time
where the time goes in v5:
time: 86.1 us; the launch traced here: 85.9 us
  Pallas kernels  84.4 us (98%)
  between operations  1.48 us (2%)
    pallas_call x1, Pallas kernels, on_device(): pl.pallas_call(gather_kernel, out_shape=(jax.ShapeDtypeStruct((NX, NZ, NY...  39.2 us
    pallas_call x1, Pallas kernels, on_device(): pl.pallas_call(update_kernel, out_shape=(jax.ShapeDtypeStruct((ROWS, R),...  36 us
    pallas_call x1, Pallas kernels, on_device(): pl.pallas_call(inverse_kernel, out_shape=(jax.ShapeDtypeStruct((R, R), F3...  6.09 us
    pallas_call x1, Pallas kernels, on_device(): pl.pallas_call(pick_kernel, out_shape=(jax.ShapeDtypeStruct((ROWS, R), BF...  3.1 us

profile of v5, /device:TPU:2, one launch (start us, length us, event | category | flops | bytes accessed | tf_op | source)
XLA Modules:
  0.0 85.9 jit_solution(11259216531043676635)
XLA Ops:
  0.6 0.0 copy-start
  1.4 39.2 %gather_factors.1 = (bf16[4,16,4,2,16,256]{5,4,3,2,1,0:T(8,128)(2,1)S(1)}, bf16[256,256]{1,0:T(8,128)(2,1)S(1)}, f32[256,256]{1,0:T(8,128)S(1)}) custom-call(bf16[64,256]{1,0:T(8,128)(2,1)} %b_ref.1, bf16[256,256]{1,0:T(8,128)(2,1)} %c_ref.1), custom_call_target="tpu_custom_call" | custom-call | tf_op jit(solution)/shard_map/gather_factors/pallas_call | solution.py:470
  40.7 6.1 %invert_select.1 = (f32[256,256]{1,0:T(8,128)S(1)}, f32[6,64,256]{2,1,0:T(8,128)S(1)}, bf16[6,64,256]{2,1,0:T(8,128)(2,1)S(1)}, s32[6,2,8,256]{3,2,1,0:T(8,128)S(1)}) custom-call(s32[1,1]{1,0:T(1,128)S(6)} %copy.10.counts_ref, s32[1,1,6]{2,1,0:T(1,128)} %row_hbm.1, s32[1,1,6]{2,1,0:T(1,128)} %col_hbm.1, s32[1,1,6]{2,1,0:T(1,128)} %depth_hbm.1, ...), custom_call_target="tpu_custom_call" | custom-call | tf_op jit(solution)/shard_map/invert_select/pallas_call | solution.py:489
  46.8 0.0 copy-start.1
  46.8 0.0 copy-done
  46.8 36.0 %update_gather.1 = (bf16[32,256]{1,0:T(8,128)(2,1)S(1)}, bf16[4,16,2,32,256]{4,3,2,1,0:T(8,128)(2,1)S(1)}) custom-call(bf16[1,1,6,64,4096]{4,3,2,1,0:T(8,128)(2,1)S(1)} %copy-done, f32[6,64,256]{2,1,0:T(8,128)S(1)} %get-tuple-element.14.rows_b_ref, bf16[6,64,256]{2,1,0:T(8,128)(2,1)S(1)} %get-tuple-element.15.rows_c_ref, ...), custom_call_target="tpu_custom_call" | custom-call | tf_op jit(solution)/shard_map/update_gather/pallas_call | solution.py:503
  82.8 0.0 copy-done.1
  82.8 3.1 %pick_units.1 = (bf16[32,256]{1,0:T(8,128)(2,1)}, bf16[1,1,64,4096]{3,2,1,0:T(8,128)(2,1)}) custom-call(s32[1,1,64]{2,1,0:T(1,128)S(1)} %copy-done.1, bf16[32,256]{1,0:T(8,128)(2,1)S(1)} %get-tuple-element.18.solved_ref, bf16[4,16,2,32,256]{4,3,2,1,0:T(8,128)(2,1)S(1)} %get-tuple-element.19.full), custom_call_target="tpu_custom_call" | custom-call | tf_op jit(solution)/shard_map/pick_units/pallas_call | solution.py:523
Async XLA Ops:
  0.6 46.2 %copy-start = (bf16[1,1,6,64,4096]{4,3,2,1,0:T(8,128)(2,1)S(1)}, bf16[1,1,6,64,4096]{4,3,2,1,0:T(8,128)(2,1)}, u32[]{:S(2)}) copy-start(bf16[1,1,6,64,4096]{4,3,2,1,0:T(8,128)(2,1)} %values_ref.1) | copy-start | bytes 9437188
  46.8 36.0 %copy-start.1 = (s32[1,1,64]{2,1,0:T(1,128)S(1)}, s32[1,1,64]{2,1,0:T(1,128)}, u32[]{:S(2)}) copy-start(s32[1,1,64]{2,1,0:T(1,128)} %fetch_ref.1) | copy-start | bytes 772
